TPU v7x, 32 devices: a whole 2x2x4 slice. The times are simulated.
32 devices in a mesh: dp: 4 (over z), seq: 8 (over y, x, core).
Axes of the slice: x: 2, y: 2, z: 4, core: 2. Of those that a mesh axis runs over, the one named last changes fastest.
Arguments:
- queries: bfloat16 [32, 2, 128, 4096], P(('dp', 'seq')), parts along dimension 0, may hold values from -6 to 6
- key_heads: bfloat16 [32, 2, 128, 512], P(('dp', 'seq')), parts along dimension 0, may hold values from -6 to 6
- value_heads: bfloat16 [32, 2, 128, 512], P(('dp', 'seq')), parts along dimension 0, may hold values from -6 to 6
- out_grad: bfloat16 [32, 2, 128, 4096], P(('dp', 'seq')), parts along dimension 0, may hold values from -6 to 6
- doc_lengths: int32 [32], P('dp'), parts along dimension 0, may hold values from 1 to 384, 2048 in all
- block_reach: int32 [64], P('dp'), parts along dimension 0, may hold values from 0 to 3, as said below
Outputs:
- attended: bfloat16 [32, 2, 128, 4096], P(('dp', 'seq')), parts along dimension 0
- query_grad: bfloat16 [32, 2, 128, 4096], P(('dp', 'seq')), parts along dimension 0
- key_grad: bfloat16 [32, 2, 128, 512], P(('dp', 'seq')), parts along dimension 0
- value_grad: bfloat16 [32, 2, 128, 512], P(('dp', 'seq')), parts along dimension 0
There are 4 independent parts, one for each index of `dp`. A program takes and returns all parts, laid end to end along the dimension named above; each array names one. Nothing has to cross between parts.
Inputs may be any that keep to these rules, and one draw needn't show every extreme that they name: doc_lengths are positive, sum to 2048, and the longest is exactly 384. `block_reach`: the value 4 - 1 occurs in every draw.
All inputs are finite; a program needn't handle non-finite values.
Results may differ from a plain program's by a relative error of at most 0.025.
Values may be sent and summed in bfloat16 or wider, within the bound.
A program may use at most 128 MiB of HBM per device.

v0:
```python
import jax
import jax.numpy as jnp
from jax import lax
from jax.sharding import PartitionSpec as P

HEAD_SIZE = 128
WIN = 4


masked_fill = -1e30


def shifted(shard, axis, by):
    length = lax.axis_size(axis)
    pairs = [(i, i + by) for i in range(length) if 0 <= i + by < length]
    return lax.ppermute(shard, axis, pairs)


def doc_index(positions, doc_ends):
    return jnp.sum((positions[:, None] >= doc_ends[None, :]).astype(jnp.int32), axis=1)


def attend(queries_blk, grads_blk, window, first_key, block_index, reach_now, doc_ends):
    block_rows = queries_blk.shape[0]
    key_rows = window.shape[0]
    kv_width = window.shape[1] // 2
    heads_kv = kv_width // HEAD_SIZE
    group_size = queries_blk.shape[1] // kv_width
    score_scale = HEAD_SIZE ** (-0.5)
    q_four = queries_blk.reshape(block_rows, heads_kv, group_size, HEAD_SIZE)
    g_four = grads_blk.reshape(block_rows, heads_kv, group_size, HEAD_SIZE)
    k_three = window[:, :kv_width].reshape(key_rows, heads_kv, HEAD_SIZE)
    v_three = window[:, kv_width:].reshape(key_rows, heads_kv, HEAD_SIZE)
    query_pos = block_index * block_rows + jnp.arange(block_rows, dtype=jnp.int32)
    key_pos = first_key + jnp.arange(key_rows, dtype=jnp.int32)
    allowed = (key_pos[None, :] <= query_pos[:, None]) & (key_pos[None, :] >= 0)
    allowed = allowed & (
        doc_index(key_pos, doc_ends)[None, :] == doc_index(query_pos, doc_ends)[:, None]
    )
    allowed = allowed & (key_pos[None, :] // block_rows >= block_index - reach_now)
    scores = (
        jnp.einsum("tkgd,skd->kgts", q_four, k_three, preferred_element_type=jnp.float32)
        * score_scale
    )
    masked = jnp.where(allowed, scores, masked_fill)
    row_max = jnp.max(masked, axis=-1, keepdims=True)
    row_sum = jnp.sum(jnp.exp(masked - row_max), axis=-1, keepdims=True)
    log_total = row_max + jnp.log(row_sum)
    weights = jnp.exp(masked - log_total)
    weights_low = weights.astype(jnp.bfloat16)
    attended = jnp.einsum(
        "kgts,skd->tkgd", weights_low, v_three, preferred_element_type=jnp.float32
    ).astype(jnp.bfloat16)
    row_delta = jnp.einsum("tkgd,tkgd->kgt", g_four, attended, preferred_element_type=jnp.float32)
    weight_grad = jnp.einsum("tkgd,skd->kgts", g_four, v_three, preferred_element_type=jnp.float32)
    score_grad = (weights * (weight_grad - row_delta[..., None]) * score_scale).astype(jnp.bfloat16)
    query_grad = jnp.einsum(
        "kgts,skd->tkgd", score_grad, k_three, preferred_element_type=jnp.float32
    ).astype(jnp.bfloat16)
    key_part = jnp.einsum("kgts,tkgd->skd", score_grad, q_four, preferred_element_type=jnp.float32)
    value_part = jnp.einsum(
        "kgts,tkgd->skd", weights_low, g_four, preferred_element_type=jnp.float32
    )
    partials = jnp.concatenate(
        [key_part.reshape(key_rows, kv_width), value_part.reshape(key_rows, kv_width)], axis=1
    )
    return (attended.reshape(block_rows, -1), query_grad.reshape(block_rows, -1), partials)


def window_hops(own_low, own_high, device_index, seq_devices):
    last_device = device_index == seq_devices - 1
    blocks_low = [own_low]
    blocks_high = [own_high]
    current_low, current_high = (own_low, own_high)
    for hop_index in range(WIN - 1):
        from_below = shifted(current_low, "seq", 1)
        from_above = shifted(current_high, "seq", -1)
        current_high = jnp.where(last_device, current_low, from_above)
        current_low = from_below
        blocks_low.insert(0, current_low)
        blocks_high.insert(0, current_high)
    return (jnp.concatenate(blocks_low, axis=0), jnp.concatenate(blocks_high, axis=0))


def return_hops(partial_low, partial_high, device_index, seq_devices, block_rows):
    last_device = device_index == seq_devices - 1
    total_low = partial_low[:block_rows]
    total_high = partial_high[:block_rows]
    for hop_index in range(1, WIN):
        from_above = shifted(total_low, "seq", -1)
        from_below = shifted(total_high, "seq", 1)
        from_above = jnp.where(last_device, total_high, from_above)
        total_low = from_above + partial_low[hop_index * block_rows : (hop_index + 1) * block_rows]
        total_high = (
            from_below + partial_high[hop_index * block_rows : (hop_index + 1) * block_rows]
        )
    return (total_low, total_high)


def shards(queries, key_heads, value_heads, out_grad, doc_lengths, block_reach):
    seq_devices = lax.axis_size("seq")
    device_index = lax.axis_index("seq")
    block_rows = queries.shape[2]
    kv_width = key_heads.shape[3]
    doc_ends = jnp.cumsum(doc_lengths)
    own_blocks = jnp.concatenate([key_heads[0], value_heads[0]], axis=-1)
    window_low, window_high = window_hops(own_blocks[0], own_blocks[1], device_index, seq_devices)
    block_high = 2 * seq_devices - 1 - device_index
    results = []
    for slot_index, block_index, window in (
        (0, device_index, window_low),
        (1, block_high, window_high),
    ):
        reach_now = lax.dynamic_index_in_dim(block_reach, block_index, keepdims=False)
        outcome = attend(
            queries[0, slot_index],
            out_grad[0, slot_index],
            window,
            (block_index - WIN + 1) * block_rows,
            block_index,
            reach_now,
            doc_ends,
        )
        results.append(outcome)
    total_low, total_high = return_hops(
        results[0][2], results[1][2], device_index, seq_devices, block_rows
    )
    attended = jnp.stack([results[0][0], results[1][0]], axis=0)[None]
    query_grad = jnp.stack([results[0][1], results[1][1]], axis=0)[None]
    gradients = jnp.stack([total_low, total_high], axis=0)[None]
    key_grad = gradients[..., :kv_width].astype(jnp.bfloat16)
    value_grad = gradients[..., kv_width:].astype(jnp.bfloat16)
    return (attended, query_grad, key_grad, value_grad)


def solution(mesh):
    in_specs = (
        P(("dp", "seq"), None, None, None),
        P(("dp", "seq"), None, None, None),
        P(("dp", "seq"), None, None, None),
        P(("dp", "seq"), None, None, None),
        P("dp"),
        P("dp"),
    )
    out_specs = (
        P(("dp", "seq"), None, None, None),
        P(("dp", "seq"), None, None, None),
        P(("dp", "seq"), None, None, None),
        P(("dp", "seq"), None, None, None),
    )
    return jax.shard_map(shards, mesh=mesh, in_specs=in_specs, out_specs=out_specs, check_vma=False)
```

profile of v0, /device:TPU:28, one launch (start us, length us, event | category | flops | bytes accessed | tf_op | source)
XLA Modules:
  0.0 134.2 jit_solution(7586596902393759037)
XLA Ops:
  0.7 1.1 copy.64
  1.8 1.1 copy.65
  2.9 2.8 %collective-permute-start.3 = (bf16[128,1024]{0,1:T(8,128)(2,1)S(1)}, bf16[128,1024]{0,1:T(8,128)(2,1)}, u32[]{:S(2)}, u32[]{:S(2)}) collective-permute-start(bf16[128,1024]{0,1:T(8,128)(2,1)S(1)} %fusion.29), channel_id=1, source_target_pairs={{1,0},{2,1},{3,2},{4,3},{5,4},{6,5},{7,6},{9,8},{10,9},{11,10},{12... | collective-permute-start | bytes 786440 | tf_op jit(solution)/shard_map/ppermute | solution.py:16
  5.8 2.7 %fusion.59 = (bf16[1,1,128,4096]{3,2,1,0:T(8,128)(2,1)S(1)}, bf16[1,1,128,4096]{3,2,1,0:T(8,128)(2,1)}) fusion(bf16[1,2,128,4096]{3,2,1,0:T(8,128)(2,1)} %param.6), kind=kLoop, calls=%fused_computation.112 | loop fusion | bytes 4194304 | tf_op jit(solution)/shard_map/slice | solution.py:116
  8.5 2.7 %fusion.58 = (bf16[1,1,128,4096]{3,2,1,0:T(8,128)(2,1)}, bf16[1,1,128,4096]{3,2,1,0:T(8,128)(2,1)S(1)}) fusion(bf16[1,2,128,4096]{3,2,1,0:T(8,128)(2,1)} %param.9), kind=kLoop, calls=%fused_computation.111 | loop fusion | bytes 4194304 | tf_op jit(solution)/shard_map/slice | solution.py:117
  11.2 0.6 fusion.63
  12.5 1.1 broadcast_select_fusion.2
  13.5 2.6 %collective-permute-start.4 = (bf16[128,1024]{0,1:T(8,128)(2,1)S(1)}, bf16[128,1024]{0,1:T(8,128)(2,1)S(1)}, u32[]{:S(2)}, u32[]{:S(2)}) collective-permute-start(bf16[128,1024]{0,1:T(8,128)(2,1)S(1)} %get-tuple-element.22), channel_id=1, source_target_pairs={{1,0},{2,1},{3,2},{4,3},{5,4},{6,5},{7,6},{9,8},{10,9},{11,10},{12... | collective-permute-start | bytes 786440 | tf_op jit(solution)/shard_map/ppermute | solution.py:16
  16.1 1.9 %collective-permute-start = (bf16[128,1024]{0,1:T(8,128)(2,1)S(1)}, bf16[128,1024]{0,1:T(8,128)(2,1)}, u32[]{:S(2)}, u32[]{:S(2)}) collective-permute-start(bf16[128,1024]{0,1:T(8,128)(2,1)S(1)} %get-tuple-element.23), channel_id=1, source_target_pairs={{0,1},{1,2},{2,3},{3,4},{4,5},{5,6},{6,7},{8,9},{9,10},{10,11},{11... | collective-permute-start | bytes 786440 | tf_op jit(solution)/shard_map/ppermute | solution.py:16
  18.7 0.2 reduce-window.8
  18.9 0.1 convert_reduce_fusion.3
  19.0 0.1 convert_reduce_fusion.1
  19.1 1.7 %collective-permute-done.4 = bf16[128,1024]{0,1:T(8,128)(2,1)S(1)} collective-permute-done((bf16[128,1024]{0,1:T(8,128)(2,1)S(1)}, bf16[128,1024]{0,1:T(8,128)(2,1)S(1)}, u32[]{:S(2)}, u32[]{:S(2)}) %collective-permute-start.4) | collective-permute-done | bytes 262176 | tf_op jit(solution)/shard_map/ppermute | solution.py:16
  20.8 4.0 %collective-permute-done = bf16[128,1024]{0,1:T(8,128)(2,1)} collective-permute-done((bf16[128,1024]{0,1:T(8,128)(2,1)S(1)}, bf16[128,1024]{0,1:T(8,128)(2,1)}, u32[]{:S(2)}, u32[]{:S(2)}) %collective-permute-start) | collective-permute-done | bytes 262176 | tf_op jit(solution)/shard_map/ppermute | solution.py:16
  24.8 0.7 broadcast_select_fusion.1
  25.6 1.9 %collective-permute-start.5 = (bf16[128,1024]{0,1:T(8,128)(2,1)}, bf16[128,1024]{0,1:T(8,128)(2,1)}, u32[]{:S(2)}, u32[]{:S(2)}) collective-permute-start(bf16[128,1024]{0,1:T(8,128)(2,1)} %broadcast_select_fusion.1), channel_id=1, source_target_pairs={{1,0},{2,1},{3,2},{4,3},{5,4},{6,5},{7,6},{9,8},{10,9},{11,10},{12... | collective-permute-start | bytes 786440 | tf_op jit(solution)/shard_map/ppermute | solution.py:16
  27.5 2.4 %collective-permute-start.1 = (bf16[128,1024]{0,1:T(8,128)(2,1)}, bf16[128,1024]{0,1:T(8,128)(2,1)}, u32[]{:S(2)}, u32[]{:S(2)}) collective-permute-start(bf16[128,1024]{0,1:T(8,128)(2,1)} %collective-permute-done), channel_id=1, source_target_pairs={{0,1},{1,2},{2,3},{3,4},{4,5},{5,6},{6,7},{8,9},{9,10},{10,11},{11... | collective-permute-start | bytes 786440 | tf_op jit(solution)/shard_map/ppermute | solution.py:16
  29.9 0.7 copy.138
  30.6 1.6 %copy.139 = bf16[1,1,128,4096]{2,3,1,0:T(8,128)(2,1)S(1)} copy(bf16[1,1,128,4096]{3,2,1,0:T(8,128)(2,1)} %get-tuple-element.27) | data formatting | bytes 2097152
  32.2 2.3 %copy.140 = bf16[1,1,128,4096]{2,3,1,0:T(8,128)(2,1)} copy(bf16[1,1,128,4096]{3,2,1,0:T(8,128)(2,1)} %get-tuple-element.24) | data formatting | bytes 2097152
  34.5 1.3 copy.141
  35.8 0.7 and_and_fusion
  36.5 1.0 broadcast_select_fusion
  37.5 1.1 pad_maximum_fusion.1
  38.7 0.1 fusion.61
  38.8 1.4 %fusion.9 = (f32[4,8,128]{2,1,0:T(8,128)S(1)}, f32[4,512,128,8]{2,1,3,0:T(8,128)S(1)}) fusion(pred[128,512]{0,1:T(8,128)(4,1)S(1)} %get-tuple-element.44, bf16[512,4,128,1]{0,2,3,1:T(8,128)(2,1)S(1)} %bitcast.187, bf16[128,4,8,128]{0,3,2,1:T(8,128)(2,1)S(1)} %bitcast.175), kind=kOutput, calls=%fused_computation.17 | convolution fusion | flops 543158272 | bytes 10043392 | tf_op jit(solution)/shard_map/tkgd,skd->kgts/dot_general | solution.py:42
  40.2 1.8 %exponential_reduce_fusion = f32[4,8,128]{2,1,0:T(8,128)S(1)} fusion(f32[4,512,128,8]{2,1,3,0:T(8,128)S(1)} %get-tuple-element.37, f32[4,8,128]{2,1,0:T(8,128)S(1)} %get-tuple-element.36, pred[128,512]{0,1:T(8,128)(4,1)S(1)} %get-tuple-element.44), kind=kLoop, calls=%fused_computation.11 | loop fusion | flops 8384512 | bytes 8486912 | tf_op jit(solution)/shard_map/reduce_sum | solution.py:47
  42.1 3.3 %fusion.10 = (f32[4,8,128]{2,1,0:T(8,128)S(1)}, bf16[4,128,8,128]{3,1,2,0:T(8,128)(2,1)}) fusion(bf16[4,8,128,128]{2,3,1,0:T(8,128)(2,1)S(1)} %bitcast.199, bf16[512,4,128,1]{0,2,3,1:T(8,128)(2,1)S(1)} %bitcast.205, f32[4,512,128,8]{2,1,3,0:T(8,128)S(1)} %get-tuple-element.37, f32[4,8,128]{2,1,0:T(8,128)S(1)} %log_add_fusion, ...), kind=kOutput, calls=%fused_computation.33 | convolution fusion | flops 547876864 | bytes 11108352 | tf_op jit(solution)/shard_map/kgts,skd->tkgd/dot_general | solution.py:51
  45.4 2.3 %collective-permute-start.2 = (bf16[128,1024]{0,1:T(8,128)(2,1)}, bf16[128,1024]{0,1:T(8,128)(2,1)S(1)}, u32[]{:S(2)}, u32[]{:S(2)}) collective-permute-start(bf16[128,1024]{0,1:T(8,128)(2,1)} %collective-permute-done.1), channel_id=1, source_target_pairs={{0,1},{1,2},{2,3},{3,4},{4,5},{5,6},{6,7},{8,9},{9,10},{10,11},{11... | collective-permute-start | bytes 786440 | tf_op jit(solution)/shard_map/ppermute | solution.py:16
  47.6 3.2 %fusion.2 = bf16[4,8,128,512]{2,3,1,0:T(8,128)(2,1)S(1)} fusion(f32[4,512,128,8]{2,1,3,0:T(8,128)S(1)} %get-tuple-element.37, f32[4,8,128]{2,1,0:T(8,128)S(1)} %get-tuple-element.40, f32[4,8,128]{2,1,0:T(8,128)S(1)} %log_add_fusion, pred[128,512]{0,1:T(8,128)(4,1)S(1)} %get-tuple-element.44, bf16[512,4,128,1]{0,2,3,1:T(8,128)(2,1)S(1)} %bitcast.206, ...), kind=kOutput, calls=%fused_computation.3 | convolution fusion | flops 551550976 | bytes 14254080 | tf_op jit(solution)/shard_map/tkgd,skd->kgts/dot_general | solution.py:55
  50.8 3.3 %collective-permute-done.2 = bf16[128,1024]{0,1:T(8,128)(2,1)S(1)} collective-permute-done((bf16[128,1024]{0,1:T(8,128)(2,1)}, bf16[128,1024]{0,1:T(8,128)(2,1)S(1)}, u32[]{:S(2)}, u32[]{:S(2)}) %collective-permute-start.2) | collective-permute-done | bytes 262176 | tf_op jit(solution)/shard_map/ppermute | solution.py:16
  54.1 1.1 pad_maximum_fusion
  55.4 1.4 %fusion.8 = (f32[4,8,128]{2,1,0:T(8,128)S(1)}, f32[4,512,128,8]{2,1,3,0:T(8,128)S(1)}) fusion(pred[128,512]{0,1:T(8,128)(4,1)S(1)} %get-tuple-element.45, bf16[512,4,128,1]{0,2,3,1:T(8,128)(2,1)S(1)} %bitcast.189, bf16[128,4,8,128]{0,3,2,1:T(8,128)(2,1)S(1)} %bitcast.177), kind=kOutput, calls=%fused_computation.16 | convolution fusion | flops 543158272 | bytes 10043392 | tf_op jit(solution)/shard_map/tkgd,skd->kgts/dot_general | solution.py:42
  56.8 1.8 %exponential_reduce_fusion.1 = f32[4,8,128]{2,1,0:T(8,128)S(1)} fusion(f32[4,512,128,8]{2,1,3,0:T(8,128)S(1)} %get-tuple-element.39, f32[4,8,128]{2,1,0:T(8,128)S(1)} %get-tuple-element.38, pred[128,512]{0,1:T(8,128)(4,1)S(1)} %get-tuple-element.45), kind=kLoop, calls=%fused_computation.13 | loop fusion | flops 8384512 | bytes 8486912 | tf_op jit(solution)/shard_map/reduce_sum | solution.py:47
  58.7 3.2 %fusion.33 = f32[4,512,128,1]{1,2,3,0:T(8,128)} fusion(bf16[128,4,8,128]{0,3,2,1:T(8,128)(2,1)S(1)} %bitcast.202, f32[4,512,128,8]{2,1,3,0:T(8,128)S(1)} %get-tuple-element.39, f32[4,8,128]{2,1,0:T(8,128)S(1)} %log_add_fusion.1, pred[128,512]{0,1:T(8,128)(4,1)S(1)} %get-tuple-element.45), kind=kOutput, calls=%fused_computation.72 | convolution fusion | flops 545259520 | bytes 10567680 | tf_op jit(solution)/shard_map/kgts,tkgd->skd/dot_general | solution.py:61
  61.9 3.3 %fusion.11 = (f32[4,8,128]{2,1,0:T(8,128)S(1)}, bf16[4,128,8,128]{3,1,2,0:T(8,128)(2,1)}) fusion(bf16[4,8,128,128]{2,3,1,0:T(8,128)(2,1)S(1)} %bitcast.203, bf16[512,4,128,1]{0,2,3,1:T(8,128)(2,1)S(1)} %bitcast.207, f32[4,512,128,8]{2,1,3,0:T(8,128)S(1)} %get-tuple-element.39, f32[4,8,128]{2,1,0:T(8,128)S(1)} %log_add_fusion.1, ...), kind=kOutput, calls=%fused_computation.35 | convolution fusion | flops 547876864 | bytes 11108352 | tf_op jit(solution)/shard_map/kgts,skd->tkgd/dot_general | solution.py:51
  65.1 4.3 %fusion.5 = bf16[4,8,128,512]{2,3,1,0:T(8,128)(2,1)S(1)} fusion(f32[4,512,128,8]{2,1,3,0:T(8,128)S(1)} %get-tuple-element.39, f32[4,8,128]{2,1,0:T(8,128)S(1)} %get-tuple-element.42, f32[4,8,128]{2,1,0:T(8,128)S(1)} %log_add_fusion.1, pred[128,512]{0,1:T(8,128)(4,1)S(1)} %get-tuple-element.45, bf16[512,4,128,1]{0,2,3,1:T(8,128)(2,1)} %bitcast.208, ...), kind=kOutput, calls=%fused_computation.7 | convolution fusion | flops 551550976 | bytes 14254080 | tf_op jit(solution)/shard_map/tkgd,skd->kgts/dot_general | solution.py:55
  69.5 1.5 %fusion.65 = f32[4,512,128,1]{1,2,3,0:T(8,128)S(1)} fusion(bf16[4,8,128,512]{2,3,1,0:T(8,128)(2,1)S(1)} %fusion.5, bf16[128,4,8,128]{0,3,2,1:T(8,128)(2,1)S(1)} %bitcast.178), kind=kOutput, calls=%fused_computation.118 | convolution fusion | flops 536870912 | bytes 6291456 | tf_op jit(solution)/shard_map/kgts,tkgd->skd/dot_general | solution.py:60
  71.0 0.5 copy-done.1
  71.5 2.3 %collective-permute-start.8 = (f32[128,1024]{0,1:T(8,128)S(1)}, f32[128,1024]{0,1:T(8,128)S(1)}, u32[]{:S(2)}, u32[]{:S(2)}) collective-permute-start(f32[128,1024]{0,1:T(8,128)S(1)} %fusion.15), channel_id=1, source_target_pairs={{1,0},{2,1},{3,2},{4,3},{5,4},{6,5},{7,6},{9,8},{10,9},{11,10},{12... | collective-permute-start | bytes 1572872 | tf_op jit(solution)/shard_map/ppermute | solution.py:16
  73.8 2.2 %fusion.30 = f32[4,512,128,1]{1,2,3,0:T(8,128)S(1)} fusion(bf16[128,4,8,128]{0,3,2,1:T(8,128)(2,1)S(1)} %bitcast.201, f32[4,512,128,8]{2,1,3,0:T(8,128)S(1)} %get-tuple-element.37, f32[4,8,128]{2,1,0:T(8,128)S(1)} %log_add_fusion, pred[128,512]{0,1:T(8,128)(4,1)S(1)} %get-tuple-element.44), kind=kOutput, calls=%fused_computation.71 | convolution fusion | flops 545259520 | bytes 10567680 | tf_op jit(solution)/shard_map/kgts,tkgd->skd/dot_general | solution.py:61
  76.0 1.5 %fusion.64 = f32[4,512,128,1]{1,2,3,0:T(8,128)S(1)} fusion(bf16[4,8,128,512]{2,3,1,0:T(8,128)(2,1)S(1)} %fusion.2, bf16[128,4,8,128]{0,3,2,1:T(8,128)(2,1)S(1)} %bitcast.176), kind=kOutput, calls=%fused_computation.117 | convolution fusion | flops 536870912 | bytes 6291456 | tf_op jit(solution)/shard_map/kgts,tkgd->skd/dot_general | solution.py:60
  77.5 2.8 %collective-permute-done.8 = f32[128,1024]{0,1:T(8,128)S(1)} collective-permute-done((f32[128,1024]{0,1:T(8,128)S(1)}, f32[128,1024]{0,1:T(8,128)S(1)}, u32[]{:S(2)}, u32[]{:S(2)}) %collective-permute-start.8) | collective-permute-done | bytes 524320 | tf_op jit(solution)/shard_map/ppermute | solution.py:16
  80.3 0.1 fusion.17
  80.4 4.7 %collective-permute-start.9 = (f32[128,1024]{0,1:T(8,128)S(1)}, f32[128,1024]{0,1:T(8,128)S(1)}, u32[]{:S(2)}, u32[]{:S(2)}) collective-permute-start(f32[128,1024]{0,1:T(8,128)S(1)} %get-tuple-element.20), channel_id=1, source_target_pairs={{1,0},{2,1},{3,2},{4,3},{5,4},{6,5},{7,6},{9,8},{10,9},{11,10},{12... | collective-permute-start | bytes 1572872 | tf_op jit(solution)/shard_map/ppermute | solution.py:16
  85.1 1.9 %collective-permute-start.6 = (f32[128,1024]{0,1:T(8,128)S(1)}, f32[128,1024]{0,1:T(8,128)S(1)}, u32[]{:S(2)}, u32[]{:S(2)}) collective-permute-start(f32[128,1024]{0,1:T(8,128)S(1)} %get-tuple-element.21), channel_id=1, source_target_pairs={{0,1},{1,2},{2,3},{3,4},{4,5},{5,6},{6,7},{8,9},{9,10},{10,11},{11... | collective-permute-start | bytes 1572872 | tf_op jit(solution)/shard_map/ppermute | solution.py:16
  87.0 9.6 %collective-permute-done.9 = f32[128,1024]{0,1:T(8,128)S(1)} collective-permute-done((f32[128,1024]{0,1:T(8,128)S(1)}, f32[128,1024]{0,1:T(8,128)S(1)}, u32[]{:S(2)}, u32[]{:S(2)}) %collective-permute-start.9) | collective-permute-done | bytes 524320 | tf_op jit(solution)/shard_map/ppermute | solution.py:16
  96.6 1.1 fusion.14
  97.7 4.7 %collective-permute-start.10 = (f32[128,1024]{0,1:T(8,128)}, f32[128,1024]{0,1:T(8,128)}, u32[]{:S(2)}, u32[]{:S(2)}) collective-permute-start(f32[128,1024]{0,1:T(8,128)} %get-tuple-element.18), channel_id=1, source_target_pairs={{1,0},{2,1},{3,2},{4,3},{5,4},{6,5},{7,6},{9,8},{10,9},{11,10},{12... | collective-permute-start | bytes 1572872 | tf_op jit(solution)/shard_map/ppermute | solution.py:16
  102.4 1.9 %collective-permute-start.7 = (f32[128,1024]{0,1:T(8,128)}, f32[128,1024]{0,1:T(8,128)}, u32[]{:S(2)}, u32[]{:S(2)}) collective-permute-start(f32[128,1024]{0,1:T(8,128)} %get-tuple-element.19), channel_id=1, source_target_pairs={{0,1},{1,2},{2,3},{3,4},{4,5},{5,6},{6,7},{8,9},{9,10},{10,11},{11... | collective-permute-start | bytes 1572872 | tf_op jit(solution)/shard_map/ppermute | solution.py:16
  104.4 1.7 %convolution_convert_fusion = bf16[4,128,8,128]{3,1,2,0:T(8,128)(2,1)} fusion(bf16[512,4,128,1]{0,2,3,1:T(8,128)(2,1)S(1)} %bitcast.188, bf16[4,8,128,512]{2,3,1,0:T(8,128)(2,1)S(1)} %fusion.2), kind=kOutput, calls=%fused_computation.36 | convolution fusion | flops 537395200 | bytes 5767168 | tf_op jit(solution)/shard_map/kgts,skd->tkgd/dot_general | solution.py:57
  106.1 2.4 %copy.85 = bf16[1,128,4096]{2,1,0:T(8,128)(2,1)} copy(bf16[1,128,4096]{1,2,0:T(8,128)(2,1)} %bitcast.191) | data formatting | bytes 2097152 | tf_op jit(solution)/shard_map/stack;reshape | solution.py:129
  108.5 2.3 %copy.75 = bf16[1,128,4096]{2,1,0:T(8,128)(2,1)} copy(bf16[1,128,4096]{1,2,0:T(8,128)(2,1)} %bitcast.197) | data formatting | bytes 2097152 | tf_op jit(solution)/shard_map/stack;reshape | solution.py:128
  110.8 4.1 %convolution_convert_fusion.1 = bf16[4,128,8,128]{3,1,2,0:T(8,128)(2,1)} fusion(bf16[512,4,128,1]{0,2,3,1:T(8,128)(2,1)} %bitcast.190, bf16[4,8,128,512]{2,3,1,0:T(8,128)(2,1)} %copy-done), kind=kOutput, calls=%fused_computation.37 | convolution fusion | flops 537395200 | bytes 5767168 | tf_op jit(solution)/shard_map/kgts,skd->tkgd/dot_general | solution.py:57
  114.9 2.3 %copy.84 = bf16[1,128,4096]{2,1,0:T(8,128)(2,1)} copy(bf16[1,128,4096]{1,2,0:T(8,128)(2,1)} %bitcast.192) | data formatting | bytes 2097152 | tf_op jit(solution)/shard_map/stack;reshape | solution.py:129
  117.2 2.2 %fusion.26 = (bf16[1,128,1024]{1,2,0:T(8,128)(2,1)S(1)}, f32[128,1024]{0,1:T(8,128)}) fusion(f32[512,512]{0,1:T(8,128)S(1)} %bitcast.182, f32[512,512]{0,1:T(8,128)S(1)} %bitcast.170, f32[128,1024]{0,1:T(8,128)} %collective-permute-done.10, pred[]{:T(512)S(6)} %eq.33, f32[128,1024]{0,1:T(8,128)} %collective-permute-done.7, f32[512,512]{0,1:T(8,128)} %bitcast.185, ...), kind=kLoop, calls=%fused_computation.59 | loop fusion | flops 786432 | bytes 6029313 | tf_op jit(solution)/shard_map/stack | solution.py:130
  119.4 2.6 %collective-permute-start.11 = (f32[128,1024]{0,1:T(8,128)}, f32[128,1024]{0,1:T(8,128)}, u32[]{:S(2)}, u32[]{:S(2)}) collective-permute-start(f32[128,1024]{0,1:T(8,128)} %get-tuple-element.17), channel_id=1, source_target_pairs={{0,1},{1,2},{2,3},{3,4},{4,5},{5,6},{6,7},{8,9},{9,10},{10,11},{11... | collective-permute-start | bytes 1572872 | tf_op jit(solution)/shard_map/ppermute | solution.py:16
  122.0 3.1 %maximum_bitcast_fusion.1 = bf16[1,2,128,4096]{3,2,1,0:T(8,128)(2,1)} fusion(bf16[1,128,4096]{2,1,0:T(8,128)(2,1)} %copy.85, bf16[1,128,4096]{2,1,0:T(8,128)(2,1)} %copy.84), kind=kLoop, calls=%fused_computation.31 | loop fusion | flops 1048576 | bytes 4194304 | tf_op jit(solution)/shard_map/broadcast_in_dim | solution.py:129
  125.0 1.5 %copy.74 = bf16[1,128,4096]{2,1,0:T(8,128)(2,1)S(1)} copy(bf16[1,128,4096]{1,2,0:T(8,128)(2,1)} %bitcast.198) | data formatting | bytes 2097152 | tf_op jit(solution)/shard_map/stack;reshape | solution.py:128
  126.5 2.7 %maximum_bitcast_fusion = bf16[1,2,128,4096]{3,2,1,0:T(8,128)(2,1)} fusion(bf16[1,128,4096]{2,1,0:T(8,128)(2,1)} %copy.75, bf16[1,128,4096]{2,1,0:T(8,128)(2,1)S(1)} %copy.74), kind=kLoop, calls=%fused_computation.30 | loop fusion | flops 1048576 | bytes 4194304 | tf_op jit(solution)/shard_map/broadcast_in_dim | solution.py:128
  129.3 1.9 %collective-permute-done.11 = f32[128,1024]{0,1:T(8,128)} collective-permute-done((f32[128,1024]{0,1:T(8,128)}, f32[128,1024]{0,1:T(8,128)}, u32[]{:S(2)}, u32[]{:S(2)}) %collective-permute-start.11) | collective-permute-done | bytes 524320 | tf_op jit(solution)/shard_map/ppermute | solution.py:16
  131.2 1.1 fusion.24
  132.5 0.9 copy.91
  133.3 0.8 copy.90
  (54 shorter events, 0.4 us)
Async XLA Ops:
  0.6 10.6 %copy-start.15 = (s32[16]{0:T(128)S(1)}, s32[16]{0:T(128)}, u32[]{:S(2)}) copy-start(s32[16]{0:T(128)} %param.11) | copy-start | bytes 196
  0.6 18.1 %copy-start.16 = (s32[8]{0:T(128)S(1)}, s32[8]{0:T(128)}, u32[]{:S(2)}) copy-start(s32[8]{0:T(128)} %param.10) | copy-start | bytes 100
  2.9 9.5 %collective-permute-start.3 = (bf16[128,1024]{0,1:T(8,128)(2,1)S(1)}, bf16[128,1024]{0,1:T(8,128)(2,1)}, u32[]{:S(2)}, u32[]{:S(2)}) collective-permute-start(bf16[128,1024]{0,1:T(8,128)(2,1)S(1)} %fusion.29), channel_id=1, source_target_pairs={{1,0},{2,1},{3,2},{4,3},{5,4},{6,5},{7,6},{9,8},{10,9},{11,10},{12... | collective-permute-start | bytes 786440 | tf_op jit(solution)/shard_map/ppermute | solution.py:16
  13.5 16.4 %copy-start.11 = (bf16[128,1024]{0,1:T(8,128)(2,1)}, bf16[128,1024]{0,1:T(8,128)(2,1)S(1)}, u32[]{:S(2)}) copy-start(bf16[128,1024]{0,1:T(8,128)(2,1)S(1)} %get-tuple-element.23) | copy-start | bytes 786436
  13.5 16.4 %copy-start.13 = (bf16[128,1024]{0,1:T(8,128)(2,1)}, bf16[128,1024]{0,1:T(8,128)(2,1)S(1)}, u32[]{:S(2)}) copy-start(bf16[128,1024]{0,1:T(8,128)(2,1)S(1)} %get-tuple-element.22) | copy-start | bytes 786436
  13.5 7.3 %collective-permute-start.4 = (bf16[128,1024]{0,1:T(8,128)(2,1)S(1)}, bf16[128,1024]{0,1:T(8,128)(2,1)S(1)}, u32[]{:S(2)}, u32[]{:S(2)}) collective-permute-start(bf16[128,1024]{0,1:T(8,128)(2,1)S(1)} %get-tuple-element.22), channel_id=1, source_target_pairs={{1,0},{2,1},{3,2},{4,3},{5,4},{6,5},{7,6},{9,8},{10,9},{11,10},{12... | collective-permute-start | bytes 786440 | tf_op jit(solution)/shard_map/ppermute | solution.py:16
  16.1 8.7 %collective-permute-start = (bf16[128,1024]{0,1:T(8,128)(2,1)S(1)}, bf16[128,1024]{0,1:T(8,128)(2,1)}, u32[]{:S(2)}, u32[]{:S(2)}) collective-permute-start(bf16[128,1024]{0,1:T(8,128)(2,1)S(1)} %get-tuple-element.23), channel_id=1, source_target_pairs={{0,1},{1,2},{2,3},{3,4},{4,5},{5,6},{6,7},{8,9},{9,10},{10,11},{11... | collective-permute-start | bytes 786440 | tf_op jit(solution)/shard_map/ppermute | solution.py:16
  25.6 11.0 %collective-permute-start.5 = (bf16[128,1024]{0,1:T(8,128)(2,1)}, bf16[128,1024]{0,1:T(8,128)(2,1)}, u32[]{:S(2)}, u32[]{:S(2)}) collective-permute-start(bf16[128,1024]{0,1:T(8,128)(2,1)} %broadcast_select_fusion.1), channel_id=1, source_target_pairs={{1,0},{2,1},{3,2},{4,3},{5,4},{6,5},{7,6},{9,8},{10,9},{11,10},{12... | collective-permute-start | bytes 786440 | tf_op jit(solution)/shard_map/ppermute | solution.py:16
  27.5 9.1 %collective-permute-start.1 = (bf16[128,1024]{0,1:T(8,128)(2,1)}, bf16[128,1024]{0,1:T(8,128)(2,1)}, u32[]{:S(2)}, u32[]{:S(2)}) collective-permute-start(bf16[128,1024]{0,1:T(8,128)(2,1)} %collective-permute-done), channel_id=1, source_target_pairs={{0,1},{1,2},{2,3},{3,4},{4,5},{5,6},{6,7},{8,9},{9,10},{10,11},{11... | collective-permute-start | bytes 786440 | tf_op jit(solution)/shard_map/ppermute | solution.py:16
  38.8 3.3 %copy-start.5 = (bf16[512,512]{0,1:T(8,128)(2,1)}, bf16[512,512]{0,1:T(8,128)(2,1)S(1)}, u32[]{:S(2)}) copy-start(bf16[512,512]{0,1:T(8,128)(2,1)S(1)} %get-tuple-element.30) | copy-start | bytes 1572868
  38.8 3.3 %copy-start.8 = (bf16[1,1,128,4096]{2,3,1,0:T(8,128)(2,1)S(1)}, bf16[1,1,128,4096]{2,3,1,0:T(8,128)(2,1)}, u32[]{:S(2)}) copy-start(bf16[1,1,128,4096]{2,3,1,0:T(8,128)(2,1)} %copy.141) | copy-start | bytes 3145732
  45.4 8.8 %collective-permute-start.2 = (bf16[128,1024]{0,1:T(8,128)(2,1)}, bf16[128,1024]{0,1:T(8,128)(2,1)S(1)}, u32[]{:S(2)}, u32[]{:S(2)}) collective-permute-start(bf16[128,1024]{0,1:T(8,128)(2,1)} %collective-permute-done.1), channel_id=1, source_target_pairs={{0,1},{1,2},{2,3},{3,4},{4,5},{5,6},{6,7},{8,9},{9,10},{10,11},{11... | collective-permute-start | bytes 786440 | tf_op jit(solution)/shard_map/ppermute | solution.py:16
  47.6 6.5 %copy-start.12 = (bf16[128,1024]{0,1:T(8,128)(2,1)S(1)}, bf16[128,1024]{0,1:T(8,128)(2,1)}, u32[]{:S(2)}) copy-start(bf16[128,1024]{0,1:T(8,128)(2,1)} %copy-done.11) | copy-start | bytes 786436
  55.4 3.3 %copy-start.7 = (bf16[512,512]{0,1:T(8,128)(2,1)}, bf16[512,512]{0,1:T(8,128)(2,1)S(1)}, u32[]{:S(2)}) copy-start(bf16[512,512]{0,1:T(8,128)(2,1)S(1)} %get-tuple-element.28) | copy-start | bytes 1572868
  55.4 6.5 %copy-start.14 = (bf16[512,512]{0,1:T(8,128)(2,1)}, bf16[512,512]{0,1:T(8,128)(2,1)S(1)}, u32[]{:S(2)}) copy-start(bf16[512,512]{0,1:T(8,128)(2,1)S(1)} %get-tuple-element.29) | copy-start | bytes 1572868
  55.4 3.3 %copy-start.10 = (bf16[1,1,128,4096]{2,3,1,0:T(8,128)(2,1)S(1)}, bf16[1,1,128,4096]{2,3,1,0:T(8,128)(2,1)}, u32[]{:S(2)}) copy-start(bf16[1,1,128,4096]{2,3,1,0:T(8,128)(2,1)} %copy.140) | copy-start | bytes 3145732
  69.4 6.5 %copy-start = (bf16[4,8,128,512]{2,3,1,0:T(8,128)(2,1)}, bf16[4,8,128,512]{2,3,1,0:T(8,128)(2,1)S(1)}, u32[]{:S(2)}) copy-start(bf16[4,8,128,512]{2,3,1,0:T(8,128)(2,1)S(1)} %fusion.5) | copy-start | bytes 12582916
  69.5 2.0 %copy-start.1 = (f32[4,512,128,1]{1,2,3,0:T(8,128)S(1)}, f32[4,512,128,1]{1,2,3,0:T(8,128)}, u32[]{:S(2)}) copy-start(f32[4,512,128,1]{1,2,3,0:T(8,128)} %fusion.33) | copy-start | bytes 3145732
  69.5 4.4 %copy-start.9 = (bf16[1,1,128,4096]{2,3,1,0:T(8,128)(2,1)S(1)}, bf16[1,1,128,4096]{2,3,1,0:T(8,128)(2,1)}, u32[]{:S(2)}) copy-start(bf16[1,1,128,4096]{2,3,1,0:T(8,128)(2,1)} %copy.141) | copy-start | bytes 3145732
  71.5 8.7 %collective-permute-start.8 = (f32[128,1024]{0,1:T(8,128)S(1)}, f32[128,1024]{0,1:T(8,128)S(1)}, u32[]{:S(2)}, u32[]{:S(2)}) collective-permute-start(f32[128,1024]{0,1:T(8,128)S(1)} %fusion.15), channel_id=1, source_target_pairs={{1,0},{2,1},{3,2},{4,3},{5,4},{6,5},{7,6},{9,8},{10,9},{11,10},{12... | collective-permute-start | bytes 1572872 | tf_op jit(solution)/shard_map/ppermute | solution.py:16
  76.0 21.7 %copy-start.3 = (f32[4,512,128,1]{1,2,3,0:T(8,128)}, f32[4,512,128,1]{1,2,3,0:T(8,128)S(1)}, u32[]{:S(2)}) copy-start(f32[4,512,128,1]{1,2,3,0:T(8,128)S(1)} %fusion.30) | copy-start | bytes 3145732
  77.5 26.9 %copy-start.6 = (bf16[512,512]{0,1:T(8,128)(2,1)S(1)}, bf16[512,512]{0,1:T(8,128)(2,1)}, u32[]{:S(2)}) copy-start(bf16[512,512]{0,1:T(8,128)(2,1)} %copy-done.5) | copy-start | bytes 1572868
  80.4 16.2 %collective-permute-start.9 = (f32[128,1024]{0,1:T(8,128)S(1)}, f32[128,1024]{0,1:T(8,128)S(1)}, u32[]{:S(2)}, u32[]{:S(2)}) collective-permute-start(f32[128,1024]{0,1:T(8,128)S(1)} %get-tuple-element.20), channel_id=1, source_target_pairs={{1,0},{2,1},{3,2},{4,3},{5,4},{6,5},{7,6},{9,8},{10,9},{11,10},{12... | collective-permute-start | bytes 1572872 | tf_op jit(solution)/shard_map/ppermute | solution.py:16
  85.1 11.5 %collective-permute-start.6 = (f32[128,1024]{0,1:T(8,128)S(1)}, f32[128,1024]{0,1:T(8,128)S(1)}, u32[]{:S(2)}, u32[]{:S(2)}) collective-permute-start(f32[128,1024]{0,1:T(8,128)S(1)} %get-tuple-element.21), channel_id=1, source_target_pairs={{0,1},{1,2},{2,3},{3,4},{4,5},{5,6},{6,7},{8,9},{9,10},{10,11},{11... | collective-permute-start | bytes 1572872 | tf_op jit(solution)/shard_map/ppermute | solution.py:16
  97.7 19.5 %collective-permute-start.10 = (f32[128,1024]{0,1:T(8,128)}, f32[128,1024]{0,1:T(8,128)}, u32[]{:S(2)}, u32[]{:S(2)}) collective-permute-start(f32[128,1024]{0,1:T(8,128)} %get-tuple-element.18), channel_id=1, source_target_pairs={{1,0},{2,1},{3,2},{4,3},{5,4},{6,5},{7,6},{9,8},{10,9},{11,10},{12... | collective-permute-start | bytes 1572872 | tf_op jit(solution)/shard_map/ppermute | solution.py:16
  102.4 14.8 %collective-permute-start.7 = (f32[128,1024]{0,1:T(8,128)}, f32[128,1024]{0,1:T(8,128)}, u32[]{:S(2)}, u32[]{:S(2)}) collective-permute-start(f32[128,1024]{0,1:T(8,128)} %get-tuple-element.19), channel_id=1, source_target_pairs={{0,1},{1,2},{2,3},{3,4},{4,5},{5,6},{6,7},{8,9},{9,10},{10,11},{11... | collective-permute-start | bytes 1572872 | tf_op jit(solution)/shard_map/ppermute | solution.py:16
  106.1 11.1 %copy-start.2 = (f32[4,512,128,1]{1,2,3,0:T(8,128)S(1)}, f32[4,512,128,1]{1,2,3,0:T(8,128)}, u32[]{:S(2)}) copy-start(f32[4,512,128,1]{1,2,3,0:T(8,128)} %fusion.33) | copy-start | bytes 3145732
  119.4 11.8 %copy-start.4 = (f32[4,512,128,1]{1,2,3,0:T(8,128)S(1)}, f32[4,512,128,1]{1,2,3,0:T(8,128)}, u32[]{:S(2)}) copy-start(f32[4,512,128,1]{1,2,3,0:T(8,128)} %copy-done.3) | copy-start | bytes 3145732
  119.4 11.8 %collective-permute-start.11 = (f32[128,1024]{0,1:T(8,128)}, f32[128,1024]{0,1:T(8,128)}, u32[]{:S(2)}, u32[]{:S(2)}) collective-permute-start(f32[128,1024]{0,1:T(8,128)} %get-tuple-element.17), channel_id=1, source_target_pairs={{0,1},{1,2},{2,3},{3,4},{4,5},{5,6},{6,7},{8,9},{9,10},{10,11},{11... | collective-permute-start | bytes 1572872 | tf_op jit(solution)/shard_map/ppermute | solution.py:16
where the time goes:
time: 135 us; the launch traced here: 134 us
  starting transfers between devices  32 us (24%)
  matrix products  31 us (23%)
  local copies, waits for them, and re-layouts  25 us (19%)
  waiting for transfers between devices  23.3 us (17%)
  other arithmetic  20.3 us (15%)
  between operations  2.51 us (2%)
    ppermute x12, starting transfers between devices, shifted(): return lax.ppermute(shard, axis, pairs)  32 us
    ppermute x12, waiting for transfers between devices, shifted(): return lax.ppermute(shard, axis, pairs)  23.3 us
    unnamed x42, local copies, waits for them, and re-layouts  10.4 us
    dot_general x2, matrix products, attend(): jnp.einsum('tkgd,skd->kgts', g_four, v_three, preferred_element_type=jnp....  7.5 us
    dot_general x2, matrix products, attend(): jnp.einsum('kgts,skd->tkgd', weights_low, v_three, preferred_element_type...  6.55 us
    dot_general x2, matrix products, attend(): jnp.einsum('kgts,skd->tkgd', score_grad, k_three, preferred_element_type=...  5.82 us
    dot_general x2, matrix products, attend(): jnp.einsum('kgts,tkgd->skd', weights_low, g_four, preferred_element_type=...  5.34 us
    another operation x2, local copies, waits for them, and re-layouts, shards(): query_grad = jnp.stack([results[0][1], results[1][1]], axis=0)[None]  4.67 us
  transfers between devices with their start and end apart: 12, of which 6 were waited for; matrix products, arithmetic and copies ran while one was open for 30% of the time, Pallas kernels for 0%

commit v1 on v0

v1 whole, which is shorter than its diff:
```python
import functools

import jax
import jax.numpy as jnp
from jax import lax
from jax.experimental import pallas as pl
from jax.experimental.pallas import tpu as pltpu
from jax.sharding import PartitionSpec as P

HEAD_SIZE = 128
WIN = 4
NEG = -1e30
LOG2E = 1.4426950408889634
MESH = pl.DeviceIdType.MESH


def kernel(n, heads_kv, group, rows, docs,
           len_ref, reach_ref, q_hbm, k_hbm, v_hbm, g_hbm,
           att_hbm, dq_hbm, dk_ref, dv_ref,
           win, q_s, g_s, att_s, dq_s, bias, p_s, ds_s, acc, pout, s1, fin,
           own_sem, in_sem, out_sem, kv_send, kv_recv, p_send, p_recv):
    d = lax.axis_index("seq")
    odd = lax.rem(d, 2) == 1
    even = jnp.logical_not(odd)
    sib = d + 1 - 2 * lax.rem(d, 2)
    width = group * HEAD_SIZE
    scale = HEAD_SIZE ** (-0.5)

    def cols(h, size):
        return pl.ds(pl.multiple_of(h * size, size), size)

    def own_copy(slot, which, h):
        src = (k_hbm, v_hbm)[which]
        return pltpu.make_async_copy(
            src.at[0, slot, :, cols(h, HEAD_SIZE)], win.at[4 * slot, h, which],
            own_sem.at[slot, which, h])

    def in_copy(which, slot, h):
        src, dst = ((q_hbm, q_s), (g_hbm, g_s))[which]
        return pltpu.make_async_copy(
            src.at[0, slot, :, cols(h, width)], dst.at[h, slot], in_sem.at[which, slot, h])

    def out_copy(which, slot, h):
        src, dst = ((att_s, att_hbm), (dq_s, dq_hbm))[which]
        return pltpu.make_async_copy(
            src.at[h, slot], dst.at[0, slot, :, cols(h, width)], out_sem.at[which, slot, h])

    def remote(src, dst, send_sem, recv_sem, target):
        return pltpu.make_async_remote_copy(
            src_ref=src, dst_ref=dst, send_sem=send_sem, recv_sem=recv_sem,
            device_id={"seq": target}, device_id_type=MESH)

    def kv(src, dst, kind, h, target):
        return remote(win.at[src, h], win.at[dst, h], kv_send.at[kind, h], kv_recv.at[dst, h],
                      target)

    kv_direct = (
        (d + 2 <= n - 1, 0, 2, 0, d + 2),
        (d >= 2, 4, 6, 1, d - 2),
        (jnp.logical_and(odd, d + 3 <= n - 1), 0, 3, 2, d + 3),
        (even, 0, 1, 2, sib),
        (jnp.logical_and(even, d >= 3), 4, 7, 3, d - 3),
        (odd, 4, 5, 3, sib),
        (d == n - 1, 0, 6, 6, d - 1),
        (d == n - 1, 0, 7, 7, d - 2),
    )
    kv_relay = (
        (jnp.logical_and(even, d >= 2), 2, 3, 4, sib),
        (jnp.logical_and(odd, d >= 2), 2, 1, 4, sib),
        (jnp.logical_and(odd, d + 2 <= n - 1), 6, 7, 5, sib),
        (jnp.logical_and(even, d + 2 <= n - 1), 6, 5, 5, sib),
    )

    def start_kv(table, h):
        for cond, src, dst, kind, target in table:
            @pl.when(cond)
            def _(src=src, dst=dst, kind=kind, target=target):
                kv(src, dst, kind, h, target).start()

    def wait_kv(cond, slot, h):
        @pl.when(cond)
        def _():
            kv(slot, slot, 0, h, sib).wait_recv()

    direct_in = (
        (d >= 2, 2), (d <= n - 2, 6), (odd, 1), (jnp.logical_and(even, d >= 3), 3),
        (even, 5),
        (jnp.logical_and(odd, d <= n - 3), 7),
    )
    relay_in = (
        (jnp.logical_and(even, d >= 2), 1), (jnp.logical_and(odd, d >= 3), 3),
        (jnp.logical_and(odd, d <= n - 2), 5),
        (jnp.logical_and(even, d <= n - 4), 7),
    )

    def part(src, kind, h, target):
        dst = s1.at[kind, h] if kind < 2 else fin.at[kind - 2, h]
        return remote(pout.at[src, h], dst, p_send.at[kind, h], p_recv.at[kind, h], target)

    part_first = (
        (jnp.logical_and(even, d >= 2), 1, 0, sib),
        (jnp.logical_and(odd, d >= 2), 3, 0, sib),
        (jnp.logical_and(odd, d <= n - 3), 5, 1, sib),
        (jnp.logical_and(even, d <= n - 3), 7, 1, sib),
        (jnp.logical_and(even, d >= 3), 3, 3, d - 3),
        (odd, 1, 3, sib),
        (jnp.logical_and(odd, d + 3 <= n - 1), 7, 5, d + 3),
        (even, 5, 5, sib),
        (d == n - 2, 6, 6, sib),
        (d == n - 3, 7, 7, d + 2),
    )
    part_second = (
        (d >= 2, 2, 2, d - 2),
        (d <= n - 3, 6, 4, d + 2),
    )
    fin_in = (
        (d <= n - 3, 2),
        (jnp.logical_or(even, d + 3 <= n - 1), 3),
        (d >= 2, 4),
        (jnp.logical_or(odd, d >= 3), 5),
        (d == n - 1, 6),
        (d == n - 1, 7),
    )

    def start_part(table, h):
        for cond, src, kind, target in table:
            @pl.when(cond)
            def _(src=src, kind=kind, target=target):
                part(src, kind, h, target).start()

    def wait_part(cond, kind, h):
        @pl.when(cond)
        def _():
            part(2, kind, h, sib).wait_recv()

    for h in range(heads_kv):
        for slot in range(2):
            for which in range(2):
                own_copy(slot, which, h).start()
    for h in range(heads_kv):
        for slot in range(2):
            for which in range(2):
                in_copy(which, slot, h).start()

    for slot in (1, 2, 3, 5, 6, 7):
        win[slot] = jnp.zeros(win.shape[1:], win.dtype)
    fin[...] = jnp.zeros(fin.shape, fin.dtype)

    barrier = pltpu.get_barrier_semaphore()
    partners = (
        (d >= 0, sib), (d >= 2, d - 2), (d + 2 <= n - 1, d + 2),
        (jnp.logical_and(odd, d + 3 <= n - 1), d + 3),
        (jnp.logical_and(even, d >= 3), d - 3),
    )
    for cond, target in partners:
        @pl.when(cond)
        def _(target=target):
            pl.semaphore_signal(barrier, inc=1, device_id={"seq": target}, device_id_type=MESH)
    peers = jnp.int32(0)
    for cond, _t in partners:
        peers = peers + jnp.where(cond, 1, 0)
    pl.semaphore_wait(barrier, peers)

    for h in range(heads_kv):
        for slot in range(2):
            for which in range(2):
                own_copy(slot, which, h).wait()
        start_kv(kv_direct, h)

    for slot, block in ((0, d), (1, 2 * n - 1 - d)):
        pos = block * rows + lax.broadcasted_iota(jnp.int32, (rows, 1), 0)
        first = jnp.zeros((rows, 1), jnp.int32)
        end = jnp.int32(0)
        for i in range(docs):
            end = end + len_ref[i]
            first = jnp.where(pos >= end, end, first)
        first = jnp.maximum(first, (block - reach_ref[block]) * rows)
        key = (block - WIN + 1) * rows + lax.broadcasted_iota(jnp.int32, (rows, WIN * rows), 1)
        ok = jnp.logical_and(key <= pos, key >= first)
        bias[slot] = jnp.where(ok, 0.0, NEG)

    last = d == n - 1
    slot_of = (
        (0, 1, 2, 3),
        (4, jnp.where(last, 0, 5), jnp.where(last, 1, 6),
         jnp.where(last, 2, jnp.where(d == n - 2, 0, 7))),
    )

    def stage_second(h):
        wait_part(d >= 2, 0, h)
        wait_part(d <= n - 3, 1, h)

        @pl.when(d >= 2)
        def _():
            pout[2, h] = (acc[h, 2] + s1[0, h].astype(jnp.float32)).astype(pout.dtype)

        @pl.when(d <= n - 3)
        def _():
            pout[6, h] = (acc[h, 6] + s1[1, h].astype(jnp.float32)).astype(pout.dtype)
        start_part(part_second, h)

    def compute(h, slot):
        index = slot_of[slot]
        k_win = jnp.concatenate([win[index[3 - j], h, 0] for j in range(WIN)], axis=0)
        v_win = jnp.concatenate([win[index[3 - j], h, 1] for j in range(WIN)], axis=0)
        nt = (((1,), (1,)), ((), ()))
        for i in range(group):
            at = slice(i * HEAD_SIZE, (i + 1) * HEAD_SIZE)
            rs = slice(i * rows, (i + 1) * rows)
            q = q_s[h, slot, :, at]
            g = g_s[h, slot, :, at]
            s = lax.dot_general(q, k_win, nt, preferred_element_type=jnp.float32) + bias[slot]
            top = jnp.max(s, axis=-1, keepdims=True)
            e = jnp.exp2((s - top) * (scale * LOG2E))
            w = e * (1.0 / jnp.sum(e, axis=-1, keepdims=True))
            low = w.astype(jnp.bfloat16)
            p_s[rs, :] = low
            att = jnp.dot(low, v_win, preferred_element_type=jnp.float32).astype(jnp.bfloat16)
            att_s[h, slot, :, at] = att
            delta = jnp.sum(g.astype(jnp.float32) * att.astype(jnp.float32), axis=-1,
                            keepdims=True)
            wg = lax.dot_general(g, v_win, nt, preferred_element_type=jnp.float32)
            ds = (w * (wg - delta)).astype(jnp.bfloat16)
            ds_s[rs, :] = ds
            dq = jnp.dot(ds, k_win, preferred_element_type=jnp.float32) * scale
            dq_s[h, slot, :, at] = dq.astype(jnp.bfloat16)
        q_all = jnp.concatenate(
            [q_s[h, slot, :, i * HEAD_SIZE:(i + 1) * HEAD_SIZE] for i in range(group)], axis=0)
        g_all = jnp.concatenate(
            [g_s[h, slot, :, i * HEAD_SIZE:(i + 1) * HEAD_SIZE] for i in range(group)], axis=0)
        tn = (((0,), (0,)), ((), ()))
        dk = lax.dot_general(ds_s[...], q_all, tn, preferred_element_type=jnp.float32) * scale
        dv = lax.dot_general(p_s[...], g_all, tn, preferred_element_type=jnp.float32)
        for j in range(WIN):
            at = slice((3 - j) * rows, (4 - j) * rows)
            acc[h, index[j], 0] += dk[at]
            acc[h, index[j], 1] += dv[at]

    for cond, slot in direct_in:
        wait_kv(cond, slot, 0)
    start_kv(kv_relay, 0)

    def step(h, carry):
        @pl.when(h + 1 < heads_kv)
        def _():
            for cond, slot in direct_in:
                wait_kv(cond, slot, h + 1)
            start_kv(kv_relay, h + 1)
        for cond, slot in relay_in:
            wait_kv(cond, slot, h)
        acc[h] = jnp.zeros(acc.shape[1:], acc.dtype)
        for slot in range(2):
            in_copy(0, slot, h).wait()
            in_copy(1, slot, h).wait()
            compute(h, slot)
            out_copy(0, slot, h).start()
            out_copy(1, slot, h).start()
        for slot in (1, 3, 5, 7):
            pout[slot, h] = acc[h, slot].astype(pout.dtype)

        @pl.when(d == n - 2)
        def _():
            pout[6, h] = acc[h, 6].astype(pout.dtype)
        start_part(part_first, h)

        @pl.when(h >= 1)
        def _():
            stage_second(h - 1)
        return carry

    lax.fori_loop(0, heads_kv, step, 0)
    stage_second(heads_kv - 1)

    for h in range(heads_kv):
        for cond, kind in fin_in:
            wait_part(cond, kind, h)
        f32 = jnp.float32
        low = acc[h, 0] + (fin[0, h].astype(f32) + fin[1, h].astype(f32)) + (
            fin[4, h].astype(f32) + fin[5, h].astype(f32))
        high = acc[h, 4] + (fin[2, h].astype(f32) + fin[3, h].astype(f32))
        at = slice(h * HEAD_SIZE, (h + 1) * HEAD_SIZE)
        for slot, total in ((0, low), (1, high)):
            dk_ref[0, slot, :, at] = total[0].astype(dk_ref.dtype)
            dv_ref[0, slot, :, at] = total[1].astype(dv_ref.dtype)

    for h in range(heads_kv):
        for slot in range(2):
            for which in range(2):
                out_copy(which, slot, h).wait()
        for cond, src, dst, kind, target in kv_direct + kv_relay:
            @pl.when(cond)
            def _(src=src, dst=dst, kind=kind, target=target):
                kv(src, dst, kind, h, target).wait_send()
        for cond, src, kind, target in part_first + part_second:
            @pl.when(cond)
            def _(src=src, kind=kind, target=target):
                part(src, kind, h, target).wait_send()


def shards(queries, key_heads, value_heads, out_grad, doc_lengths, block_reach):
    n = lax.axis_size("seq")
    rows = queries.shape[2]
    heads_kv = key_heads.shape[3] // HEAD_SIZE
    group = queries.shape[3] // key_heads.shape[3]
    width = group * HEAD_SIZE
    bf, f32 = jnp.bfloat16, jnp.float32
    tile = (2, rows, HEAD_SIZE)
    any_spec = pl.BlockSpec(memory_space=pl.ANY)
    smem = pl.BlockSpec(memory_space=pltpu.SMEM)
    vmem = pl.BlockSpec(memory_space=pltpu.VMEM)
    dma = pltpu.SemaphoreType.DMA
    flops = 2 * 6 * 2 * heads_kv * group * rows * WIN * rows * HEAD_SIZE
    return pl.pallas_call(
        functools.partial(kernel, n, heads_kv, group, rows, doc_lengths.shape[0]),
        out_shape=(
            jax.ShapeDtypeStruct(queries.shape, bf),
            jax.ShapeDtypeStruct(queries.shape, bf),
            jax.ShapeDtypeStruct(key_heads.shape, bf),
            jax.ShapeDtypeStruct(value_heads.shape, bf),
        ),
        in_specs=[smem, smem, any_spec, any_spec, any_spec, any_spec],
        out_specs=(any_spec, any_spec, vmem, vmem),
        scratch_shapes=[
            pltpu.VMEM((8, heads_kv) + tile, bf),
            pltpu.VMEM((heads_kv, 2, rows, width), bf),
            pltpu.VMEM((heads_kv, 2, rows, width), bf),
            pltpu.VMEM((heads_kv, 2, rows, width), bf),
            pltpu.VMEM((heads_kv, 2, rows, width), bf),
            pltpu.VMEM((2, rows, WIN * rows), f32),
            pltpu.VMEM((group * rows, WIN * rows), bf),
            pltpu.VMEM((group * rows, WIN * rows), bf),
            pltpu.VMEM((heads_kv, 8) + tile, f32),
            pltpu.VMEM((8, heads_kv) + tile, bf),
            pltpu.VMEM((2, heads_kv) + tile, bf),
            pltpu.VMEM((6, heads_kv) + tile, bf),
            dma((2, 2, heads_kv)),
            dma((2, 2, heads_kv)),
            dma((2, 2, heads_kv)),
            dma((8, heads_kv)),
            dma((8, heads_kv)),
            dma((8, heads_kv)),
            dma((8, heads_kv)),
        ],
        compiler_params=pltpu.CompilerParams(
            collective_id=0, has_side_effects=True, vmem_limit_bytes=52 * 1024 * 1024),
        cost_estimate=pl.CostEstimate(
            flops=flops, bytes_accessed=4 * queries.size * 2,
            transcendentals=2 * heads_kv * group * rows * WIN * rows),
    )(doc_lengths, block_reach, queries, key_heads, value_heads, out_grad)


def solution(mesh):
    split = P(("dp", "seq"), None, None, None)
    return jax.shard_map(
        shards, mesh=mesh, in_specs=(split, split, split, split, P("dp"), P("dp")),
        out_specs=(split, split, split, split), check_vma=False)
```

time: 135 us -> 73.2 us (0.54)
  the two profiles are of different devices: /device:TPU:28 before, /device:TPU:0 now
where the time goes in v1:
time: 73.2 us; the launch traced here: 73 us
  Pallas kernels  63.2 us (86%)
  local copies, waits for them, and re-layouts  9.21 us (13%)
    pallas_call x1, Pallas kernels, shards(): pl.pallas_call(functools.partial(kernel, n, heads_kv, group, rows, doc_le...  63.2 us
    unnamed x14, local copies, waits for them, and re-layouts  9.21 us

profile of v1, /device:TPU:0, one launch (start us, length us, event | category | flops | bytes accessed | tf_op | source)
XLA Modules:
  0.0 73.0 jit_solution(7174685248535342865)
XLA Ops:
  0.6 0.0 copy-start
  0.6 0.9 %copy-done = bf16[1,2,128,512]{3,2,1,0:T(8,128)(2,1)S(1)} copy-done((bf16[1,2,128,512]{3,2,1,0:T(8,128)(2,1)S(1)}, bf16[1,2,128,512]{3,2,1,0:T(8,128)(2,1)}, u32[]{:S(2)}) %copy-start) | copy-done | bytes 262168
  1.6 0.0 copy-start.1
  1.6 0.9 %copy-done.1 = bf16[1,2,128,512]{3,2,1,0:T(8,128)(2,1)S(1)} copy-done((bf16[1,2,128,512]{3,2,1,0:T(8,128)(2,1)S(1)}, bf16[1,2,128,512]{3,2,1,0:T(8,128)(2,1)}, u32[]{:S(2)}) %copy-start.1) | copy-done | bytes 262168
  2.5 0.0 copy-start.2
  2.5 0.7 copy-done.2
  3.2 0.0 copy-start.3
  3.2 0.7 copy-done.3
  3.8 63.2 %shard_map.93 = (bf16[1,2,128,4096]{3,2,1,0:T(8,128)(2,1)}, bf16[1,2,128,4096]{3,2,1,0:T(8,128)(2,1)}, bf16[1,2,128,512]{3,2,1,0:T(8,128)(2,1)S(1)}, bf16[1,2,128,512]{3,2,1,0:T(8,128)(2,1)S(1)}) custom-call(s32[8]{0:T(128)S(1)} %copy-done.2, s32[16]{0:T(128)S(1)} %copy-done.3, bf16[1,2,128,4096]{3,2,1,0:T(8,128)(2,1)} %q_hbm.1, ...), custom_call_target="tpu_custom_call" | custom-call | flops 6442450944 | bytes 8388608 | tf_op jit(solution)/shard_map/pallas_call | solution.py:313
  67.0 0.0 copy-start.4
  67.0 3.3 %copy.14 = bf16[1,2,128,4096]{3,2,1,0:T(8,128)(2,1)} copy(bf16[1,2,128,4096]{3,2,1,0:T(8,128)(2,1)} %get-tuple-element.8) | data formatting | bytes 4194304
  70.3 0.0 copy-done.4
  70.3 1.3 %copy.15 = bf16[1,2,128,4096]{3,2,1,0:T(8,128)(2,1)} copy(bf16[1,2,128,4096]{3,2,1,0:T(8,128)(2,1)S(1)} %copy-done.4) | data formatting | bytes 4194304
  71.6 0.7 copy.16
  72.3 0.7 copy.17
Async XLA Ops:
  0.6 1.0 %copy-start = (bf16[1,2,128,512]{3,2,1,0:T(8,128)(2,1)S(1)}, bf16[1,2,128,512]{3,2,1,0:T(8,128)(2,1)}, u32[]{:S(2)}) copy-start(bf16[1,2,128,512]{3,2,1,0:T(8,128)(2,1)} %k_hbm.1) | copy-start | bytes 786436
  1.6 0.9 %copy-start.1 = (bf16[1,2,128,512]{3,2,1,0:T(8,128)(2,1)S(1)}, bf16[1,2,128,512]{3,2,1,0:T(8,128)(2,1)}, u32[]{:S(2)}) copy-start(bf16[1,2,128,512]{3,2,1,0:T(8,128)(2,1)} %v_hbm.1) | copy-start | bytes 786436
  2.5 0.7 copy-start.2
  3.2 0.7 copy-start.3
  67.0 3.3 %copy-start.4 = (bf16[1,2,128,4096]{3,2,1,0:T(8,128)(2,1)S(1)}, bf16[1,2,128,4096]{3,2,1,0:T(8,128)(2,1)}, u32[]{:S(2)}) copy-start(bf16[1,2,128,4096]{3,2,1,0:T(8,128)(2,1)} %get-tuple-element.9) | copy-start | bytes 6291460

commit v2 on v1

--- a/solution.py
+++ b/solution.py
@@ -17,7 +17,7 @@
 def kernel(n, heads_kv, group, rows, docs,
            len_ref, reach_ref, q_hbm, k_hbm, v_hbm, g_hbm,
            att_hbm, dq_hbm, dk_ref, dv_ref,
-           win, q_s, g_s, att_s, dq_s, bias, p_s, ds_s, acc, pout, s1, fin,
+           win, q_s, g_s, att_s, dq_s, bias, sc_s, wg_s, p_s, ds_s, acc, pout, s1, fin,
            own_sem, in_sem, out_sem, kv_send, kv_recv, p_send, p_recv):
     d = lax.axis_index("seq")
     odd = lax.rem(d, 2) == 1
@@ -199,42 +199,80 @@
             pout[6, h] = (acc[h, 6] + s1[1, h].astype(jnp.float32)).astype(pout.dtype)
         start_part(part_second, h)
 
-    def compute(h, slot):
+    nt = (((1,), (1,)), ((), ()))
+    tn = (((0,), (0,)), ((), ()))
+    f32 = jnp.float32
+    bf16 = jnp.bfloat16
+    pair = 2 if group % 2 == 0 else 1
+    units = group // pair
+    urows = pair * rows
+    trows = rows // 2
+
+    def window(h, slot, which):
         index = slot_of[slot]
-        k_win = jnp.concatenate([win[index[3 - j], h, 0] for j in range(WIN)], axis=0)
-        v_win = jnp.concatenate([win[index[3 - j], h, 1] for j in range(WIN)], axis=0)
-        nt = (((1,), (1,)), ((), ()))
-        for i in range(group):
-            at = slice(i * HEAD_SIZE, (i + 1) * HEAD_SIZE)
-            rs = slice(i * rows, (i + 1) * rows)
-            q = q_s[h, slot, :, at]
-            g = g_s[h, slot, :, at]
-            s = lax.dot_general(q, k_win, nt, preferred_element_type=jnp.float32) + bias[slot]
+        return jnp.concatenate([win[index[3 - j], h, which] for j in range(WIN)], axis=0)
+
+    def stacked(ref, h, slot, first, count):
+        return jnp.concatenate(
+            [ref[h, slot, :, i * HEAD_SIZE:(i + 1) * HEAD_SIZE]
+             for i in range(first, first + count)], axis=0)
+
+    def products(h, slot, u):
+        rs = slice(u * urows, (u + 1) * urows)
+        sc_s[slot, rs, :] = lax.dot_general(
+            stacked(q_s, h, slot, u * pair, pair), window(h, slot, 0), nt,
+            preferred_element_type=f32)
+        wg_s[slot, rs, :] = lax.dot_general(
+            stacked(g_s, h, slot, u * pair, pair), window(h, slot, 1), nt,
+            preferred_element_type=f32)
+
+    def weigh(slot, u):
+        for t in range(urows // trows):
+            rs = slice(u * urows + t * trows, u * urows + (t + 1) * trows)
+            bs = slice((t * trows) % rows, (t * trows) % rows + trows)
+            s = sc_s[slot, rs, :] + bias[slot, bs, :]
             top = jnp.max(s, axis=-1, keepdims=True)
             e = jnp.exp2((s - top) * (scale * LOG2E))
-            w = e * (1.0 / jnp.sum(e, axis=-1, keepdims=True))
-            low = w.astype(jnp.bfloat16)
-            p_s[rs, :] = low
-            att = jnp.dot(low, v_win, preferred_element_type=jnp.float32).astype(jnp.bfloat16)
-            att_s[h, slot, :, at] = att
-            delta = jnp.sum(g.astype(jnp.float32) * att.astype(jnp.float32), axis=-1,
-                            keepdims=True)
-            wg = lax.dot_general(g, v_win, nt, preferred_element_type=jnp.float32)
-            ds = (w * (wg - delta)).astype(jnp.bfloat16)
-            ds_s[rs, :] = ds
-            dq = jnp.dot(ds, k_win, preferred_element_type=jnp.float32) * scale
-            dq_s[h, slot, :, at] = dq.astype(jnp.bfloat16)
-        q_all = jnp.concatenate(
-            [q_s[h, slot, :, i * HEAD_SIZE:(i + 1) * HEAD_SIZE] for i in range(group)], axis=0)
-        g_all = jnp.concatenate(
-            [g_s[h, slot, :, i * HEAD_SIZE:(i + 1) * HEAD_SIZE] for i in range(group)], axis=0)
-        tn = (((0,), (0,)), ((), ()))
-        dk = lax.dot_general(ds_s[...], q_all, tn, preferred_element_type=jnp.float32) * scale
-        dv = lax.dot_general(p_s[...], g_all, tn, preferred_element_type=jnp.float32)
+            wg = wg_s[slot, rs, :]
+            inv = 1.0 / jnp.sum(e, axis=-1, keepdims=True)
+            delta = jnp.sum(e * wg, axis=-1, keepdims=True) * inv
+            w = e * inv
+            p_s[slot, rs, :] = w.astype(bf16)
+            ds_s[slot, rs, :] = (w * (wg - delta)).astype(bf16)
+
+    def outputs(h, slot, u):
+        rs = slice(u * urows, (u + 1) * urows)
+        att = jnp.dot(p_s[slot, rs, :], window(h, slot, 1), preferred_element_type=f32)
+        dq = jnp.dot(ds_s[slot, rs, :], window(h, slot, 0), preferred_element_type=f32) * scale
+        for i in range(pair):
+            at = slice((u * pair + i) * HEAD_SIZE, (u * pair + i + 1) * HEAD_SIZE)
+            att_s[h, slot, :, at] = att[i * rows:(i + 1) * rows].astype(bf16)
+            dq_s[h, slot, :, at] = dq[i * rows:(i + 1) * rows].astype(bf16)
+
+    def partials(h, slot):
+        index = slot_of[slot]
+        dk = lax.dot_general(ds_s[slot], stacked(q_s, h, slot, 0, group), tn,
+                             preferred_element_type=f32) * scale
+        dv = lax.dot_general(p_s[slot], stacked(g_s, h, slot, 0, group), tn,
+                             preferred_element_type=f32)
         for j in range(WIN):
             at = slice((3 - j) * rows, (4 - j) * rows)
             acc[h, index[j], 0] += dk[at]
             acc[h, index[j], 1] += dv[at]
+
+    def compute(h):
+        work = [(slot, u) for slot in range(2) for u in range(units)]
+        products(h, *work[0])
+        for i, (slot, u) in enumerate(work):
+            if i + 1 < len(work):
+                products(h, *work[i + 1])
+            weigh(slot, u)
+            if i:
+                outputs(h, *work[i - 1])
+                if work[i - 1][1] == units - 1:
+                    partials(h, 0)
+        outputs(h, *work[-1])
+        partials(h, 1)
 
     for cond, slot in direct_in:
         wait_kv(cond, slot, 0)
@@ -252,7 +290,8 @@
         for slot in range(2):
             in_copy(0, slot, h).wait()
             in_copy(1, slot, h).wait()
-            compute(h, slot)
+        compute(h)
+        for slot in range(2):
             out_copy(0, slot, h).start()
             out_copy(1, slot, h).start()
         for slot in (1, 3, 5, 7):
@@ -274,7 +313,6 @@
     for h in range(heads_kv):
         for cond, kind in fin_in:
             wait_part(cond, kind, h)
-        f32 = jnp.float32
         low = acc[h, 0] + (fin[0, h].astype(f32) + fin[1, h].astype(f32)) + (
             fin[4, h].astype(f32) + fin[5, h].astype(f32))
         high = acc[h, 4] + (fin[2, h].astype(f32) + fin[3, h].astype(f32))
@@ -305,7 +343,7 @@
     width = group * HEAD_SIZE
     bf, f32 = jnp.bfloat16, jnp.float32
     tile = (2, rows, HEAD_SIZE)
-    any_spec = pl.BlockSpec(memory_space=pl.ANY)
+    any_spec = pl.BlockSpec(memory_space=pltpu.HBM)
     smem = pl.BlockSpec(memory_space=pltpu.SMEM)
     vmem = pl.BlockSpec(memory_space=pltpu.VMEM)
     dma = pltpu.SemaphoreType.DMA
@@ -327,8 +365,10 @@
             pltpu.VMEM((heads_kv, 2, rows, width), bf),
             pltpu.VMEM((heads_kv, 2, rows, width), bf),
             pltpu.VMEM((2, rows, WIN * rows), f32),
-            pltpu.VMEM((group * rows, WIN * rows), bf),
-            pltpu.VMEM((group * rows, WIN * rows), bf),
+            pltpu.VMEM((2, group * rows, WIN * rows), f32),
+            pltpu.VMEM((2, group * rows, WIN * rows), f32),
+            pltpu.VMEM((2, group * rows, WIN * rows), bf),
+            pltpu.VMEM((2, group * rows, WIN * rows), bf),
             pltpu.VMEM((heads_kv, 8) + tile, f32),
             pltpu.VMEM((8, heads_kv) + tile, bf),
             pltpu.VMEM((2, heads_kv) + tile, bf),

time: 73.2 us -> 49.1 us (0.67)
  Pallas kernels: 63.2 us -> 39 us
    pallas_call x1, Pallas kernels: 63.2 us -> 39 us  [shards(): pl.pallas_call(functools.partial(kernel, n, heads_kv, group, rows, doc_le...]
where the time goes in v2:
time: 49.1 us; the launch traced here: 48.9 us
  Pallas kernels  39 us (79%)
  local copies, waits for them, and re-layouts  9.21 us (19%)
  between operations  0.66 us (1%)
    pallas_call x1, Pallas kernels, shards(): pl.pallas_call(functools.partial(kernel, n, heads_kv, group, rows, doc_le...  39 us
    unnamed x14, local copies, waits for them, and re-layouts  9.21 us

profile of v2, /device:TPU:0, one launch (start us, length us, event | category | flops | bytes accessed | tf_op | source)
XLA Modules:
  0.0 48.9 jit_solution(9652867991148038259)
XLA Ops:
  0.6 0.0 copy-start
  0.6 0.9 %copy-done = bf16[1,2,128,512]{3,2,1,0:T(8,128)(2,1)S(1)} copy-done((bf16[1,2,128,512]{3,2,1,0:T(8,128)(2,1)S(1)}, bf16[1,2,128,512]{3,2,1,0:T(8,128)(2,1)}, u32[]{:S(2)}) %copy-start) | copy-done | bytes 262168
  1.6 0.0 copy-start.1
  1.6 0.9 %copy-done.1 = bf16[1,2,128,512]{3,2,1,0:T(8,128)(2,1)S(1)} copy-done((bf16[1,2,128,512]{3,2,1,0:T(8,128)(2,1)S(1)}, bf16[1,2,128,512]{3,2,1,0:T(8,128)(2,1)}, u32[]{:S(2)}) %copy-start.1) | copy-done | bytes 262168
  2.5 0.0 copy-start.2
  2.5 0.7 %copy-done.2 = s32[8]{0:T(128)S(1)} copy-done((s32[8]{0:T(128)S(1)}, s32[8]{0:T(128)}, u32[]{:S(2)}) %copy-start.2) | copy-done | bytes 56
  3.2 0.0 copy-start.3
  3.2 0.7 %copy-done.3 = s32[16]{0:T(128)S(1)} copy-done((s32[16]{0:T(128)S(1)}, s32[16]{0:T(128)}, u32[]{:S(2)}) %copy-start.3) | copy-done | bytes 88
  3.8 39.0 %shard_map.93 = (bf16[1,2,128,4096]{3,2,1,0:T(8,128)(2,1)}, bf16[1,2,128,4096]{3,2,1,0:T(8,128)(2,1)}, bf16[1,2,128,512]{3,2,1,0:T(8,128)(2,1)S(1)}, bf16[1,2,128,512]{3,2,1,0:T(8,128)(2,1)S(1)}) custom-call(s32[8]{0:T(128)S(1)} %copy-done.2, s32[16]{0:T(128)S(1)} %copy-done.3, bf16[1,2,128,4096]{3,2,1,0:T(8,128)(2,1)} %q_hbm.1, ...), custom_call_target="tpu_custom_call" | custom-call | flops 6442450944 | bytes 8388608 | tf_op jit(solution)/shard_map/pallas_call | solution.py:351
  42.9 0.0 copy-start.4
  42.9 3.3 %copy.14 = bf16[1,2,128,4096]{3,2,1,0:T(8,128)(2,1)} copy(bf16[1,2,128,4096]{3,2,1,0:T(8,128)(2,1)} %get-tuple-element.8) | data formatting | bytes 4194304
  46.2 0.0 copy-done.4
  46.2 1.3 %copy.15 = bf16[1,2,128,4096]{3,2,1,0:T(8,128)(2,1)} copy(bf16[1,2,128,4096]{3,2,1,0:T(8,128)(2,1)S(1)} %copy-done.4) | data formatting | bytes 4194304
  47.5 0.7 %copy.16 = bf16[1,2,128,512]{3,2,1,0:T(8,128)(2,1)} copy(bf16[1,2,128,512]{3,2,1,0:T(8,128)(2,1)S(1)} %get-tuple-element.10) | data formatting | bytes 524288
  48.2 0.7 %copy.17 = bf16[1,2,128,512]{3,2,1,0:T(8,128)(2,1)} copy(bf16[1,2,128,512]{3,2,1,0:T(8,128)(2,1)S(1)} %get-tuple-element.11) | data formatting | bytes 524288
Async XLA Ops:
  0.6 1.0 %copy-start = (bf16[1,2,128,512]{3,2,1,0:T(8,128)(2,1)S(1)}, bf16[1,2,128,512]{3,2,1,0:T(8,128)(2,1)}, u32[]{:S(2)}) copy-start(bf16[1,2,128,512]{3,2,1,0:T(8,128)(2,1)} %k_hbm.1) | copy-start | bytes 786436
  1.6 0.9 %copy-start.1 = (bf16[1,2,128,512]{3,2,1,0:T(8,128)(2,1)S(1)}, bf16[1,2,128,512]{3,2,1,0:T(8,128)(2,1)}, u32[]{:S(2)}) copy-start(bf16[1,2,128,512]{3,2,1,0:T(8,128)(2,1)} %v_hbm.1) | copy-start | bytes 786436
  2.5 0.7 %copy-start.2 = (s32[8]{0:T(128)S(1)}, s32[8]{0:T(128)}, u32[]{:S(2)}) copy-start(s32[8]{0:T(128)} %len_ref.1) | copy-start | bytes 100
  3.2 0.7 %copy-start.3 = (s32[16]{0:T(128)S(1)}, s32[16]{0:T(128)}, u32[]{:S(2)}) copy-start(s32[16]{0:T(128)} %reach_ref.1) | copy-start | bytes 196
  42.9 3.3 %copy-start.4 = (bf16[1,2,128,4096]{3,2,1,0:T(8,128)(2,1)S(1)}, bf16[1,2,128,4096]{3,2,1,0:T(8,128)(2,1)}, u32[]{:S(2)}) copy-start(bf16[1,2,128,4096]{3,2,1,0:T(8,128)(2,1)} %get-tuple-element.9) | copy-start | bytes 6291460

commit v3 on v2

--- a/solution.py
+++ b/solution.py
@@ -97,13 +97,15 @@
         dst = s1.at[kind, h] if kind < 2 else fin.at[kind - 2, h]
         return remote(pout.at[src, h], dst, p_send.at[kind, h], p_recv.at[kind, h], target)
 
-    part_first = (
+    part_low = (
         (jnp.logical_and(even, d >= 2), 1, 0, sib),
         (jnp.logical_and(odd, d >= 2), 3, 0, sib),
+        (jnp.logical_and(even, d >= 3), 3, 3, d - 3),
+        (odd, 1, 3, sib),
+    )
+    part_high = (
         (jnp.logical_and(odd, d <= n - 3), 5, 1, sib),
         (jnp.logical_and(even, d <= n - 3), 7, 1, sib),
-        (jnp.logical_and(even, d >= 3), 3, 3, d - 3),
-        (odd, 1, 3, sib),
         (jnp.logical_and(odd, d + 3 <= n - 1), 7, 5, d + 3),
         (even, 5, 5, sib),
         (d == n - 2, 6, 6, sib),
@@ -161,11 +163,13 @@
         peers = peers + jnp.where(cond, 1, 0)
     pl.semaphore_wait(barrier, peers)
 
-    for h in range(heads_kv):
+    def send_own(h):
         for slot in range(2):
             for which in range(2):
                 own_copy(slot, which, h).wait()
         start_kv(kv_direct, h)
+
+    send_own(0)
 
     for slot, block in ((0, d), (1, 2 * n - 1 - d)):
         pos = block * rows + lax.broadcasted_iota(jnp.int32, (rows, 1), 0)
@@ -251,64 +255,92 @@
 
     def partials(h, slot):
         index = slot_of[slot]
-        dk = lax.dot_general(ds_s[slot], stacked(q_s, h, slot, 0, group), tn,
+        dk = lax.dot_general(stacked(q_s, h, slot, 0, group), ds_s[slot], tn,
                              preferred_element_type=f32) * scale
-        dv = lax.dot_general(p_s[slot], stacked(g_s, h, slot, 0, group), tn,
+        dv = lax.dot_general(stacked(g_s, h, slot, 0, group), p_s[slot], tn,
                              preferred_element_type=f32)
         for j in range(WIN):
             at = slice((3 - j) * rows, (4 - j) * rows)
-            acc[h, index[j], 0] += dk[at]
-            acc[h, index[j], 1] += dv[at]
-
-    def compute(h):
-        work = [(slot, u) for slot in range(2) for u in range(units)]
-        products(h, *work[0])
-        for i, (slot, u) in enumerate(work):
-            if i + 1 < len(work):
-                products(h, *work[i + 1])
+            acc[h, index[j], 0] += dk[:, at].T
+            acc[h, index[j], 1] += dv[:, at].T
+
+    def half(h, slot, last_head):
+        for u in range(units):
+            if u + 1 < units:
+                products(h, slot, u + 1)
+            elif slot == 1:
+                products(h, 0, 0)
             weigh(slot, u)
-            if i:
-                outputs(h, *work[i - 1])
-                if work[i - 1][1] == units - 1:
-                    partials(h, 0)
-        outputs(h, *work[-1])
-        partials(h, 1)
+            if u and not last_head:
+                outputs(h, slot, u - 1)
+        partials(h, slot)
+        if not last_head:
+            outputs(h, slot, units - 1)
+
+    def send_out(h, slot):
+        out_copy(0, slot, h).start()
+        out_copy(1, slot, h).start()
+
+    def finish(h, slot):
+        for u in range(units):
+            outputs(h, slot, u)
+        send_out(h, slot)
+
+    def cast_parts(h, slots):
+        for slot in slots:
+            pout[slot, h] = acc[h, slot].astype(pout.dtype)
 
     for cond, slot in direct_in:
         wait_kv(cond, slot, 0)
     start_kv(kv_relay, 0)
-
-    def step(h, carry):
-        @pl.when(h + 1 < heads_kv)
-        def _():
-            for cond, slot in direct_in:
-                wait_kv(cond, slot, h + 1)
-            start_kv(kv_relay, h + 1)
+    send_own(1)
+
+    def step(h, last_head):
         for cond, slot in relay_in:
             wait_kv(cond, slot, h)
+        if not last_head:
+            @pl.when(h + 2 < heads_kv)
+            def _():
+                send_own(h + 2)
         acc[h] = jnp.zeros(acc.shape[1:], acc.dtype)
         for slot in range(2):
             in_copy(0, slot, h).wait()
             in_copy(1, slot, h).wait()
-        compute(h)
-        for slot in range(2):
-            out_copy(0, slot, h).start()
-            out_copy(1, slot, h).start()
-        for slot in (1, 3, 5, 7):
-            pout[slot, h] = acc[h, slot].astype(pout.dtype)
+        products(h, 1, 0)
+        half(h, 1, last_head)
+        cast_parts(h, (5, 7))
 
         @pl.when(d == n - 2)
         def _():
             pout[6, h] = acc[h, 6].astype(pout.dtype)
-        start_part(part_first, h)
-
-        @pl.when(h >= 1)
-        def _():
+        start_part(part_high, h)
+        if last_head:
             stage_second(h - 1)
+        else:
+            send_out(h, 1)
+            for cond, slot in direct_in:
+                wait_kv(cond, slot, h + 1)
+            start_kv(kv_relay, h + 1)
+
+            @pl.when(h >= 1)
+            def _():
+                stage_second(h - 1)
+        half(h, 0, last_head)
+        cast_parts(h, (1, 3))
+        start_part(part_low, h)
+        if not last_head:
+            send_out(h, 0)
+
+    def body(h, carry):
+        step(h, False)
         return carry
 
-    lax.fori_loop(0, heads_kv, step, 0)
-    stage_second(heads_kv - 1)
+    end_head = heads_kv - 1
+    lax.fori_loop(0, end_head, body, 0)
+    step(end_head, True)
+    finish(end_head, 1)
+    stage_second(end_head)
+    finish(end_head, 0)
 
     for h in range(heads_kv):
         for cond, kind in fin_in:
@@ -329,7 +361,7 @@
             @pl.when(cond)
             def _(src=src, dst=dst, kind=kind, target=target):
                 kv(src, dst, kind, h, target).wait_send()
-        for cond, src, kind, target in part_first + part_second:
+        for cond, src, kind, target in part_low + part_high + part_second:
             @pl.when(cond)
             def _(src=src, kind=kind, target=target):
                 part(src, kind, h, target).wait_send()
@@ -382,7 +414,7 @@
             dma((8, heads_kv)),
         ],
         compiler_params=pltpu.CompilerParams(
-            collective_id=0, has_side_effects=True, vmem_limit_bytes=52 * 1024 * 1024),
+            collective_id=0, has_side_effects=True, vmem_limit_bytes=63 * 1024 * 1024),
         cost_estimate=pl.CostEstimate(
             flops=flops, bytes_accessed=4 * queries.size * 2,
             transcendentals=2 * heads_kv * group * rows * WIN * rows),

time: 49.1 us -> 42.2 us (0.86)
  Pallas kernels: 39 us -> 35.4 us
  local copies, waits for them, and re-layouts: 9.21 us -> 6.01 us
    pallas_call x1, Pallas kernels: 39 us -> 35.4 us  [shards(): pl.pallas_call(functools.partial(kernel, n, heads_kv, group, rows, doc_le...]
    unnamed x14 -> x10, local copies, waits for them, and re-layouts: 9.21 us -> 6.01 us
where the time goes in v3:
time: 42.2 us; the launch traced here: 42.1 us
  Pallas kernels  35.4 us (84%)
  local copies, waits for them, and re-layouts  6.01 us (14%)
  between operations  0.65 us (2%)
    pallas_call x1, Pallas kernels, shards(): pl.pallas_call(functools.partial(kernel, n, heads_kv, group, rows, doc_le...  35.4 us
    unnamed x10, local copies, waits for them, and re-layouts  6.01 us

profile of v3, /device:TPU:0, one launch (start us, length us, event | category | flops | bytes accessed | tf_op | source)
XLA Modules:
  0.0 42.1 jit_solution(6564019410031885157)
XLA Ops:
  0.6 35.4 %shard_map.93 = (bf16[1,2,128,4096]{3,2,1,0:T(8,128)(2,1)}, bf16[1,2,128,4096]{3,2,1,0:T(8,128)(2,1)}, bf16[1,2,128,512]{3,2,1,0:T(8,128)(2,1)}, bf16[1,2,128,512]{3,2,1,0:T(8,128)(2,1)}) custom-call(s32[8]{0:T(128)} %len_ref.1, s32[16]{0:T(128)} %reach_ref.1, bf16[1,2,128,4096]{3,2,1,0:T(8,128)(2,1)} %q_hbm.1, bf16[1,2,128,512]{3,2,1,0:T(8,128)(2,1)} %k_hbm.1, ...), custom_call_target="tpu_custom_call" | custom-call | flops 6442450944 | bytes 8388608 | tf_op jit(solution)/shard_map/pallas_call | solution.py:383
  36.0 0.0 copy-start
  36.0 3.3 %copy.14 = bf16[1,2,128,4096]{3,2,1,0:T(8,128)(2,1)} copy(bf16[1,2,128,4096]{3,2,1,0:T(8,128)(2,1)} %get-tuple-element.8) | data formatting | bytes 4194304
  39.3 0.0 copy-done
  39.3 0.0 copy-start.2
  39.3 0.0 copy-start.1
  39.3 1.3 %copy.15 = bf16[1,2,128,4096]{3,2,1,0:T(8,128)(2,1)} copy(bf16[1,2,128,4096]{3,2,1,0:T(8,128)(2,1)S(1)} %copy-done) | data formatting | bytes 4194304
  40.6 0.0 copy-done.2
  40.6 0.7 %copy.16 = bf16[1,2,128,512]{3,2,1,0:T(8,128)(2,1)} copy(bf16[1,2,128,512]{3,2,1,0:T(8,128)(2,1)S(1)} %copy-done.2) | data formatting | bytes 524288
  41.4 0.0 copy-done.1
  41.4 0.7 %copy.17 = bf16[1,2,128,512]{3,2,1,0:T(8,128)(2,1)} copy(bf16[1,2,128,512]{3,2,1,0:T(8,128)(2,1)S(1)} %copy-done.1) | data formatting | bytes 524288
Async XLA Ops:
  36.0 3.3 %copy-start = (bf16[1,2,128,4096]{3,2,1,0:T(8,128)(2,1)S(1)}, bf16[1,2,128,4096]{3,2,1,0:T(8,128)(2,1)}, u32[]{:S(2)}) copy-start(bf16[1,2,128,4096]{3,2,1,0:T(8,128)(2,1)} %get-tuple-element.9) | copy-start | bytes 6291460
  39.3 1.3 %copy-start.2 = (bf16[1,2,128,512]{3,2,1,0:T(8,128)(2,1)S(1)}, bf16[1,2,128,512]{3,2,1,0:T(8,128)(2,1)}, u32[]{:S(2)}) copy-start(bf16[1,2,128,512]{3,2,1,0:T(8,128)(2,1)} %get-tuple-element.10) | copy-start | bytes 786436
  39.3 2.0 %copy-start.1 = (bf16[1,2,128,512]{3,2,1,0:T(8,128)(2,1)S(1)}, bf16[1,2,128,512]{3,2,1,0:T(8,128)(2,1)}, u32[]{:S(2)}) copy-start(bf16[1,2,128,512]{3,2,1,0:T(8,128)(2,1)} %get-tuple-element.11) | copy-start | bytes 786436
